TPU v7x, 32 devices: a whole 2x2x4 slice. The times are simulated.
32 devices in a mesh: gx: 8 (over z, x), gy: 4 (over y, core).
Axes of the slice: x: 2, y: 2, z: 4, core: 2. Of those that a mesh axis runs over, the one named last changes fastest.
Arguments:
- tracers: float32 [2, 80, 128, 512], P(None, None, 'gx', 'gy'), may hold values from -6 to 6
- velocity: float32 [2, 80, 128, 512], P(None, None, 'gx', 'gy'), may hold values from -0.4 to 0.4
- mixing: float32 [79, 128, 512], P(None, 'gx', 'gy'), may hold values from 0.05 to 5
- levels: int32 [128, 512], P('gx', 'gy'), may hold values from 0 to 80, as said below
- surface: float32 [128, 512], P('gx', 'gy'), may hold values from -6 to 6
- transport: float32 [2, 128, 512], P(None, 'gx', 'gy'), may hold values from -1.5 to 1.5
- forcing: float32 [2, 128, 512], P(None, 'gx', 'gy'), may hold values from -1 to 1
Outputs:
- surface_next: float32 [128, 512], P('gx', 'gy')
- transport_next: float32 [2, 128, 512], P(None, 'gx', 'gy')
- mean_transport: float32 [2, 128, 512], P(None, 'gx', 'gy')
- tracers_next: float32 [2, 80, 128, 512], P(None, None, 'gx', 'gy')
Inputs may be any that keep to these rules, and one draw needn't show every extreme that they name: levels is 0 on land columns and 80 on columns that reach the full depth; other columns are shallower.
All inputs are finite; a program needn't handle non-finite values.
Results may differ from a plain program's by a relative error of at most 0.0003.
Values sent between devices are 32-bit elements; how exact they have to be, the bound alone decides.
A program may use at most 128 MiB of HBM per device.

v0:
```python
import jax
import jax.numpy as jnp
from jax import lax
from jax.sharding import PartitionSpec as P

K = 80
BT_STEPS = 24


height_rate = 0.5
gravity_rate = 0.9
advect_scale = 0.01


def with_halo(block, sides, width):
    for axis, dim in sides:
        count = lax.axis_size(axis)
        forward = [(i, i + 1) for i in range(count - 1)]
        backward = [(target, source) for source, target in forward]
        low = lax.ppermute(
            lax.slice_in_dim(block, block.shape[dim] - width, None, axis=dim), axis, forward
        )
        high = lax.ppermute(lax.slice_in_dim(block, 0, width, axis=dim), axis, backward)
        block = jnp.concatenate([low, block, high], axis=dim)
    return block


def from_behind(value, axis, steps):
    count = lax.axis_size(axis)
    leading, last = (max(0, -steps), min(count, count - steps))
    return lax.ppermute(value, axis, [(source, source + steps) for source in range(leading, last)])


def from_lower(field, axis):
    widths = [(0, 0)] * field.ndim
    widths[axis] = (1, 0)
    padded = jnp.pad(field, widths)
    return lax.slice_in_dim(padded, 0, field.shape[axis], axis=axis)


def from_upper(field, axis):
    widths = [(0, 0)] * field.ndim
    widths[axis] = (0, 1)
    padded = jnp.pad(field, widths)
    return lax.slice_in_dim(padded, 1, field.shape[axis] + 1, axis=axis)


def upwind_change(padded, speed, axis, count):
    parts = [lax.slice_in_dim(padded, offset, offset + count + 1, axis=axis) for offset in range(6)]
    plus = (
        2.0 * parts[0] - 13.0 * parts[1] + 47.0 * parts[2] + 27.0 * parts[3] - 3.0 * parts[4]
    ) / 60.0
    minus = (
        2.0 * parts[5] - 13.0 * parts[4] + 47.0 * parts[3] + 27.0 * parts[2] - 3.0 * parts[1]
    ) / 60.0
    flux = speed * jnp.where(speed > 0.0, plus, minus)
    return lax.slice_in_dim(flux, 1, count + 1, axis=axis) - lax.slice_in_dim(
        flux, 0, count, axis=axis
    )


def column_solve(source, coupling):
    depth_count = source.shape[1]
    gains = []
    values = []
    for level in range(depth_count):
        if level < depth_count - 1:
            upper = coupling[level]
        else:
            upper = jnp.zeros_like(coupling[0])
        if level == 0:
            pivot = 1.0 + upper
            value = source[:, 0] / pivot
        else:
            lower = coupling[level - 1]
            pivot = 1.0 + lower + upper - lower * gains[-1]
            value = (source[:, level] + lower * values[-1]) / pivot
        gains.append(upper / pivot)
        values.append(value)
    result = [None] * depth_count
    result[depth_count - 1] = values[depth_count - 1]
    for level in range(depth_count - 2, -1, -1):
        result[level] = values[level] + gains[level] * result[level + 1]
    return jnp.stack(result, axis=1)


def crop(field, margin):
    return field[margin : field.shape[0] - margin, margin : field.shape[1] - margin]


def per_device(tracers, velocity, mixing, levels, surface, transport, forcing):
    depth = levels.astype(jnp.float32) / K
    middle = ((jnp.arange(K, dtype=jnp.float32) + 0.5) / K)[:, None, None]
    tracer_ext = with_halo(tracers, (("gx", 2), ("gy", 3)), 3)
    margin = 1
    east_row = from_behind(depth[:1, :], "gx", -1)
    north_col = from_behind(depth[:, :1], "gy", -1)
    inner = jnp.concatenate([depth, north_col], axis=1)
    inner = jnp.concatenate([inner, jnp.pad(east_row, ((0, 0), (0, 1)))], axis=0)
    depth_ext = jnp.pad(inner, ((1, 0), (1, 0)))
    force_x = jnp.pad(forcing[0], 1)
    force_y = jnp.pad(forcing[1], 1)

    def fetch(state):
        return with_halo(state, (("gx", 1), ("gy", 2)), 1)

    east_depth_ext = jnp.minimum(depth_ext, from_upper(depth_ext, 0))
    north_depth_ext = jnp.minimum(depth_ext, from_upper(depth_ext, 1))
    east_wet_ext = (east_depth_ext > 0.0).astype(jnp.float32)
    north_wet_ext = (north_depth_ext > 0.0).astype(jnp.float32)
    east_flow = transport[0] * crop(east_wet_ext, margin)
    north_flow = transport[1] * crop(north_wet_ext, margin)
    zeros = jnp.zeros_like(surface)

    def one_round(index, carry):
        height, east_now, north_now, east_total, north_total = carry
        state = fetch(jnp.stack([height, east_now, north_now]))
        height_ext = state[0]
        east_ext = state[1]
        north_ext = state[2]
        height_ext = height_ext - height_rate * (
            east_ext - from_lower(east_ext, 0) + (north_ext - from_lower(north_ext, 1))
        )
        east_ext = east_wet_ext * (
            east_ext
            - gravity_rate * east_depth_ext * (from_upper(height_ext, 0) - height_ext)
            + height_rate * east_depth_ext * force_x
        )
        north_ext = north_wet_ext * (
            north_ext
            - gravity_rate * north_depth_ext * (from_upper(height_ext, 1) - height_ext)
            + height_rate * north_depth_ext * force_y
        )
        east_total = east_total + crop(east_ext, margin)
        north_total = north_total + crop(north_ext, margin)
        return (
            crop(height_ext, margin),
            crop(east_ext, margin),
            crop(north_ext, margin),
            east_total,
            north_total,
        )

    height, east_flow, north_flow, east_total, north_total = lax.fori_loop(
        0, BT_STEPS // margin, one_round, (surface, east_flow, north_flow, zeros, zeros)
    )
    east_mean = east_total / BT_STEPS
    north_mean = north_total / BT_STEPS
    east_depth = crop(east_depth_ext, margin)
    north_depth = crop(north_depth_ext, margin)
    east_speed = advect_scale * east_mean / jnp.maximum(east_depth, 1.0 / K)
    north_speed = advect_scale * north_mean / jnp.maximum(north_depth, 1.0 / K)
    east_face = (velocity[0] + east_speed) * (middle < east_depth).astype(jnp.float32)
    north_face = (velocity[1] + north_speed) * (middle < north_depth).astype(jnp.float32)
    west_face = from_behind(east_face[:, -1:, :], "gx", 1)
    south_face = from_behind(north_face[:, :, -1:], "gy", 1)
    east_full = jnp.concatenate([west_face, east_face], axis=1)
    north_full = jnp.concatenate([south_face, north_face], axis=2)
    rows_x = tracers.shape[2]
    rows_y = tracers.shape[3]
    change = upwind_change(tracer_ext[:, :, :, 3:-3], east_full[None], 2, rows_x) + upwind_change(
        tracer_ext[:, :, 3:-3, :], north_full[None], 3, rows_y
    )
    stepped = tracers - change
    above = jnp.arange(1, K, dtype=jnp.int32)[:, None, None] < levels[None]
    mixed = column_solve(stepped, mixing * above.astype(jnp.float32))
    return (height, jnp.stack([east_flow, north_flow]), jnp.stack([east_mean, north_mean]), mixed)


def solution(mesh):
    placed = (
        P(None, None, "gx", "gy"),
        P(None, None, "gx", "gy"),
        P(None, "gx", "gy"),
        P("gx", "gy"),
        P("gx", "gy"),
        P(None, "gx", "gy"),
        P(None, "gx", "gy"),
    )
    return jax.shard_map(
        per_device,
        mesh=mesh,
        in_specs=placed,
        out_specs=(
            P("gx", "gy"),
            P(None, "gx", "gy"),
            P(None, "gx", "gy"),
            P(None, None, "gx", "gy"),
        ),
        check_vma=False,
    )
```

profile of v0, /device:TPU:9, one launch (start us, length us, event | category | flops | bytes accessed | tf_op | source)
XLA Modules:
  0.0 569.8 jit_solution(8889226797993655512)
XLA Ops:
  12.8 3.4 collective-permute-start.7
  61.5 422.5 %while.21 = (s32[]{:T(128)}, f32[16,128]{1,0:T(8,128)S(1)}, f32[16,128]{1,0:T(8,128)S(1)}, f32[16,128]{1,0:T(8,128)S(1)}, f32[16,128]{1,0:T(8,128)S(1)}, /*index...) while((s32[]{:T(128)}, f32[16,128]{1,0:T(8,128)S(1)}, ...), condition=%wide.region_1.2_spmd.clone, body=%wide.region_0.1_spmd.clone.sunk | while | flops 123967 | bytes 412896 | solution.py:144
  72.9 4.2 collective-permute-start.3
  82.1 3.4 collective-permute-start.1
  89.3 5.4 collective-permute-start.3
  99.6 3.4 collective-permute-start.1
  106.8 5.4 collective-permute-start.3
  117.2 3.4 collective-permute-start.1
  124.4 5.4 collective-permute-start.3
  134.7 3.4 collective-permute-start.1
  142.0 5.4 collective-permute-start.3
  152.3 3.4 collective-permute-start.1
  159.5 5.4 collective-permute-start.3
  169.8 3.4 collective-permute-start.1
  177.1 5.4 collective-permute-start.3
  187.4 3.4 collective-permute-start.1
  194.6 5.4 collective-permute-start.3
  205.0 3.4 collective-permute-start.1
  212.2 5.4 collective-permute-start.3
  222.5 3.4 collective-permute-start.1
  229.7 5.4 collective-permute-start.3
  240.1 3.4 collective-permute-start.1
  247.3 5.4 collective-permute-start.3
  257.6 3.4 collective-permute-start.1
  264.9 5.4 collective-permute-start.3
  275.2 3.4 collective-permute-start.1
  282.4 5.4 collective-permute-start.3
  292.7 3.4 collective-permute-start.1
  300.0 5.4 collective-permute-start.3
  310.3 3.4 collective-permute-start.1
  317.5 5.4 collective-permute-start.3
  327.9 3.4 collective-permute-start.1
  335.1 5.4 collective-permute-start.3
  345.4 3.4 collective-permute-start.1
  352.7 5.4 collective-permute-start.3
  363.0 3.4 collective-permute-start.1
  370.2 5.4 collective-permute-start.3
  387.8 5.4 collective-permute-start.3
  405.3 5.4 collective-permute-start.3
  415.7 3.4 collective-permute-start.1
  422.9 5.4 collective-permute-start.3
  440.4 5.4 collective-permute-start.3
  458.0 5.4 collective-permute-start.3
  475.6 5.4 collective-permute-start.3
  485.6 3.4 fusion.36
  495.5 4.5 collective-permute-start.9
  535.9 4.9 fusion.26
  545.6 4.4 maximum_maximum_fusion
  (842 shorter events, 355.7 us)
Async XLA Ops:
  1.9 57.3 %collective-permute-start.4 = (f32[16,1]{1,0:T(8,128)}, f32[16,1]{1,0:T(8,128)}, u32[]{:S(2)}, u32[]{:S(2)}) collective-permute-start(f32[16,1]{1,0:T(8,128)} %bitcast.1575), channel_id=1, source_target_pairs={{1,0},{2,1},{3,2},{5,4},{6,5},{7,6},{9,8},{10,9},{11,10},{13,12},{... | collective-permute-start | bytes 200 | tf_op jit(solution)/shard_map/ppermute | solution.py:31
  5.2 54.0 %collective-permute-start.5 = (f32[1,128]{1,0:T(1,128)S(1)}, f32[1,128]{1,0:T(1,128)S(1)}, u32[]{:S(2)}, u32[]{:S(2)}) collective-permute-start(f32[1,128]{1,0:T(1,128)S(1)} %slice.997), channel_id=1, source_target_pairs={{4,0},{8,4},{12,8},{16,12},{20,16},{24,20},{28,24},{5,1},{9,5},{13... | collective-permute-start | bytes 1544 | tf_op jit(solution)/shard_map/ppermute | solution.py:31
  10.7 509.5 %collective-permute-start.8 = (f32[2,80,3,128]{3,2,0,1:T(4,128)}, f32[2,80,3,128]{3,2,0,1:T(4,128)}, u32[]{:S(2)}, u32[]{:S(2)}) collective-permute-start(f32[2,80,3,128]{3,2,0,1:T(4,128)} %get-tuple-element.464), channel_id=1, source_target_pairs={{4,0},{8,4},{12,8},{16,12},{20,16},{24,20},{28,24},{5,1},{9,5},{13... | collective-permute-start | bytes 737288 | tf_op jit(solution)/shard_map/ppermute | solution.py:23
  12.8 507.5 %collective-permute-start.7 = (f32[2,80,3,128]{3,2,0,1:T(4,128)}, f32[2,80,3,128]{3,2,0,1:T(4,128)}, u32[]{:S(2)}, u32[]{:S(2)}) collective-permute-start(f32[2,80,3,128]{3,2,0,1:T(4,128)} %get-tuple-element.463), channel_id=1, source_target_pairs={{0,4},{4,8},{8,12},{12,16},{16,20},{20,24},{24,28},{1,5},{5,9},{9,... | collective-permute-start | bytes 737288 | tf_op jit(solution)/shard_map/ppermute | solution.py:20
  69.6 7.5 %collective-permute-start.2 = (f32[3,18,1]{2,1,0:T(8,128)S(1)}, f32[3,18,1]{2,1,0:T(8,128)S(1)}, u32[]{:S(2)}, u32[]{:S(2)}) collective-permute-start(f32[3,18,1]{2,1,0:T(8,128)S(1)} %get-tuple-element.704), channel_id=1, source_target_pairs={{1,0},{2,1},{3,2},{5,4},{6,5},{7,6},{9,8},{10,9},{11,10},{13,12},{... | collective-permute-start | bytes 656 | tf_op jit(solution)/shard_map/while/body/eval_jaxpr/ppermute | solution.py:23
  87.4 7.3 %collective-permute-start.2 = (f32[3,18,1]{2,1,0:T(8,128)S(1)}, f32[3,18,1]{2,1,0:T(8,128)S(1)}, u32[]{:S(2)}, u32[]{:S(2)}) collective-permute-start(f32[3,18,1]{2,1,0:T(8,128)S(1)} %get-tuple-element.704), channel_id=1, source_target_pairs={{1,0},{2,1},{3,2},{5,4},{6,5},{7,6},{9,8},{10,9},{11,10},{13,12},{... | collective-permute-start | bytes 656 | tf_op jit(solution)/shard_map/while/body/eval_jaxpr/ppermute | solution.py:23
  89.3 6.4 %collective-permute-start.3 = (f32[3,18,1]{2,1,0:T(8,128)S(1)}, f32[3,18,1]{2,1,0:T(8,128)S(1)}, u32[]{:S(2)}, u32[]{:S(2)}) collective-permute-start(f32[3,18,1]{2,1,0:T(8,128)S(1)} %get-tuple-element.705), channel_id=1, source_target_pairs={{0,1},{1,2},{2,3},{4,5},{5,6},{6,7},{8,9},{9,10},{10,11},{12,13},{... | collective-permute-start | bytes 656 | tf_op jit(solution)/shard_map/while/body/eval_jaxpr/ppermute | solution.py:20
  104.9 7.3 %collective-permute-start.2 = (f32[3,18,1]{2,1,0:T(8,128)S(1)}, f32[3,18,1]{2,1,0:T(8,128)S(1)}, u32[]{:S(2)}, u32[]{:S(2)}) collective-permute-start(f32[3,18,1]{2,1,0:T(8,128)S(1)} %get-tuple-element.704), channel_id=1, source_target_pairs={{1,0},{2,1},{3,2},{5,4},{6,5},{7,6},{9,8},{10,9},{11,10},{13,12},{... | collective-permute-start | bytes 656 | tf_op jit(solution)/shard_map/while/body/eval_jaxpr/ppermute | solution.py:23
  106.8 6.4 %collective-permute-start.3 = (f32[3,18,1]{2,1,0:T(8,128)S(1)}, f32[3,18,1]{2,1,0:T(8,128)S(1)}, u32[]{:S(2)}, u32[]{:S(2)}) collective-permute-start(f32[3,18,1]{2,1,0:T(8,128)S(1)} %get-tuple-element.705), channel_id=1, source_target_pairs={{0,1},{1,2},{2,3},{4,5},{5,6},{6,7},{8,9},{9,10},{10,11},{12,13},{... | collective-permute-start | bytes 656 | tf_op jit(solution)/shard_map/while/body/eval_jaxpr/ppermute | solution.py:20
  122.5 7.3 %collective-permute-start.2 = (f32[3,18,1]{2,1,0:T(8,128)S(1)}, f32[3,18,1]{2,1,0:T(8,128)S(1)}, u32[]{:S(2)}, u32[]{:S(2)}) collective-permute-start(f32[3,18,1]{2,1,0:T(8,128)S(1)} %get-tuple-element.704), channel_id=1, source_target_pairs={{1,0},{2,1},{3,2},{5,4},{6,5},{7,6},{9,8},{10,9},{11,10},{13,12},{... | collective-permute-start | bytes 656 | tf_op jit(solution)/shard_map/while/body/eval_jaxpr/ppermute | solution.py:23
  124.4 6.4 %collective-permute-start.3 = (f32[3,18,1]{2,1,0:T(8,128)S(1)}, f32[3,18,1]{2,1,0:T(8,128)S(1)}, u32[]{:S(2)}, u32[]{:S(2)}) collective-permute-start(f32[3,18,1]{2,1,0:T(8,128)S(1)} %get-tuple-element.705), channel_id=1, source_target_pairs={{0,1},{1,2},{2,3},{4,5},{5,6},{6,7},{8,9},{9,10},{10,11},{12,13},{... | collective-permute-start | bytes 656 | tf_op jit(solution)/shard_map/while/body/eval_jaxpr/ppermute | solution.py:20
  140.0 7.3 %collective-permute-start.2 = (f32[3,18,1]{2,1,0:T(8,128)S(1)}, f32[3,18,1]{2,1,0:T(8,128)S(1)}, u32[]{:S(2)}, u32[]{:S(2)}) collective-permute-start(f32[3,18,1]{2,1,0:T(8,128)S(1)} %get-tuple-element.704), channel_id=1, source_target_pairs={{1,0},{2,1},{3,2},{5,4},{6,5},{7,6},{9,8},{10,9},{11,10},{13,12},{... | collective-permute-start | bytes 656 | tf_op jit(solution)/shard_map/while/body/eval_jaxpr/ppermute | solution.py:23
  142.0 6.4 %collective-permute-start.3 = (f32[3,18,1]{2,1,0:T(8,128)S(1)}, f32[3,18,1]{2,1,0:T(8,128)S(1)}, u32[]{:S(2)}, u32[]{:S(2)}) collective-permute-start(f32[3,18,1]{2,1,0:T(8,128)S(1)} %get-tuple-element.705), channel_id=1, source_target_pairs={{0,1},{1,2},{2,3},{4,5},{5,6},{6,7},{8,9},{9,10},{10,11},{12,13},{... | collective-permute-start | bytes 656 | tf_op jit(solution)/shard_map/while/body/eval_jaxpr/ppermute | solution.py:20
  157.6 7.3 %collective-permute-start.2 = (f32[3,18,1]{2,1,0:T(8,128)S(1)}, f32[3,18,1]{2,1,0:T(8,128)S(1)}, u32[]{:S(2)}, u32[]{:S(2)}) collective-permute-start(f32[3,18,1]{2,1,0:T(8,128)S(1)} %get-tuple-element.704), channel_id=1, source_target_pairs={{1,0},{2,1},{3,2},{5,4},{6,5},{7,6},{9,8},{10,9},{11,10},{13,12},{... | collective-permute-start | bytes 656 | tf_op jit(solution)/shard_map/while/body/eval_jaxpr/ppermute | solution.py:23
  159.5 6.4 %collective-permute-start.3 = (f32[3,18,1]{2,1,0:T(8,128)S(1)}, f32[3,18,1]{2,1,0:T(8,128)S(1)}, u32[]{:S(2)}, u32[]{:S(2)}) collective-permute-start(f32[3,18,1]{2,1,0:T(8,128)S(1)} %get-tuple-element.705), channel_id=1, source_target_pairs={{0,1},{1,2},{2,3},{4,5},{5,6},{6,7},{8,9},{9,10},{10,11},{12,13},{... | collective-permute-start | bytes 656 | tf_op jit(solution)/shard_map/while/body/eval_jaxpr/ppermute | solution.py:20
  175.2 7.3 %collective-permute-start.2 = (f32[3,18,1]{2,1,0:T(8,128)S(1)}, f32[3,18,1]{2,1,0:T(8,128)S(1)}, u32[]{:S(2)}, u32[]{:S(2)}) collective-permute-start(f32[3,18,1]{2,1,0:T(8,128)S(1)} %get-tuple-element.704), channel_id=1, source_target_pairs={{1,0},{2,1},{3,2},{5,4},{6,5},{7,6},{9,8},{10,9},{11,10},{13,12},{... | collective-permute-start | bytes 656 | tf_op jit(solution)/shard_map/while/body/eval_jaxpr/ppermute | solution.py:23
  177.1 6.4 %collective-permute-start.3 = (f32[3,18,1]{2,1,0:T(8,128)S(1)}, f32[3,18,1]{2,1,0:T(8,128)S(1)}, u32[]{:S(2)}, u32[]{:S(2)}) collective-permute-start(f32[3,18,1]{2,1,0:T(8,128)S(1)} %get-tuple-element.705), channel_id=1, source_target_pairs={{0,1},{1,2},{2,3},{4,5},{5,6},{6,7},{8,9},{9,10},{10,11},{12,13},{... | collective-permute-start | bytes 656 | tf_op jit(solution)/shard_map/while/body/eval_jaxpr/ppermute | solution.py:20
  192.7 7.3 %collective-permute-start.2 = (f32[3,18,1]{2,1,0:T(8,128)S(1)}, f32[3,18,1]{2,1,0:T(8,128)S(1)}, u32[]{:S(2)}, u32[]{:S(2)}) collective-permute-start(f32[3,18,1]{2,1,0:T(8,128)S(1)} %get-tuple-element.704), channel_id=1, source_target_pairs={{1,0},{2,1},{3,2},{5,4},{6,5},{7,6},{9,8},{10,9},{11,10},{13,12},{... | collective-permute-start | bytes 656 | tf_op jit(solution)/shard_map/while/body/eval_jaxpr/ppermute | solution.py:23
  194.6 6.4 %collective-permute-start.3 = (f32[3,18,1]{2,1,0:T(8,128)S(1)}, f32[3,18,1]{2,1,0:T(8,128)S(1)}, u32[]{:S(2)}, u32[]{:S(2)}) collective-permute-start(f32[3,18,1]{2,1,0:T(8,128)S(1)} %get-tuple-element.705), channel_id=1, source_target_pairs={{0,1},{1,2},{2,3},{4,5},{5,6},{6,7},{8,9},{9,10},{10,11},{12,13},{... | collective-permute-start | bytes 656 | tf_op jit(solution)/shard_map/while/body/eval_jaxpr/ppermute | solution.py:20
  210.3 7.3 %collective-permute-start.2 = (f32[3,18,1]{2,1,0:T(8,128)S(1)}, f32[3,18,1]{2,1,0:T(8,128)S(1)}, u32[]{:S(2)}, u32[]{:S(2)}) collective-permute-start(f32[3,18,1]{2,1,0:T(8,128)S(1)} %get-tuple-element.704), channel_id=1, source_target_pairs={{1,0},{2,1},{3,2},{5,4},{6,5},{7,6},{9,8},{10,9},{11,10},{13,12},{... | collective-permute-start | bytes 656 | tf_op jit(solution)/shard_map/while/body/eval_jaxpr/ppermute | solution.py:23
  212.2 6.4 %collective-permute-start.3 = (f32[3,18,1]{2,1,0:T(8,128)S(1)}, f32[3,18,1]{2,1,0:T(8,128)S(1)}, u32[]{:S(2)}, u32[]{:S(2)}) collective-permute-start(f32[3,18,1]{2,1,0:T(8,128)S(1)} %get-tuple-element.705), channel_id=1, source_target_pairs={{0,1},{1,2},{2,3},{4,5},{5,6},{6,7},{8,9},{9,10},{10,11},{12,13},{... | collective-permute-start | bytes 656 | tf_op jit(solution)/shard_map/while/body/eval_jaxpr/ppermute | solution.py:20
  227.8 7.3 %collective-permute-start.2 = (f32[3,18,1]{2,1,0:T(8,128)S(1)}, f32[3,18,1]{2,1,0:T(8,128)S(1)}, u32[]{:S(2)}, u32[]{:S(2)}) collective-permute-start(f32[3,18,1]{2,1,0:T(8,128)S(1)} %get-tuple-element.704), channel_id=1, source_target_pairs={{1,0},{2,1},{3,2},{5,4},{6,5},{7,6},{9,8},{10,9},{11,10},{13,12},{... | collective-permute-start | bytes 656 | tf_op jit(solution)/shard_map/while/body/eval_jaxpr/ppermute | solution.py:23
  229.7 6.4 %collective-permute-start.3 = (f32[3,18,1]{2,1,0:T(8,128)S(1)}, f32[3,18,1]{2,1,0:T(8,128)S(1)}, u32[]{:S(2)}, u32[]{:S(2)}) collective-permute-start(f32[3,18,1]{2,1,0:T(8,128)S(1)} %get-tuple-element.705), channel_id=1, source_target_pairs={{0,1},{1,2},{2,3},{4,5},{5,6},{6,7},{8,9},{9,10},{10,11},{12,13},{... | collective-permute-start | bytes 656 | tf_op jit(solution)/shard_map/while/body/eval_jaxpr/ppermute | solution.py:20
  245.4 7.3 %collective-permute-start.2 = (f32[3,18,1]{2,1,0:T(8,128)S(1)}, f32[3,18,1]{2,1,0:T(8,128)S(1)}, u32[]{:S(2)}, u32[]{:S(2)}) collective-permute-start(f32[3,18,1]{2,1,0:T(8,128)S(1)} %get-tuple-element.704), channel_id=1, source_target_pairs={{1,0},{2,1},{3,2},{5,4},{6,5},{7,6},{9,8},{10,9},{11,10},{13,12},{... | collective-permute-start | bytes 656 | tf_op jit(solution)/shard_map/while/body/eval_jaxpr/ppermute | solution.py:23
  262.9 7.3 %collective-permute-start.2 = (f32[3,18,1]{2,1,0:T(8,128)S(1)}, f32[3,18,1]{2,1,0:T(8,128)S(1)}, u32[]{:S(2)}, u32[]{:S(2)}) collective-permute-start(f32[3,18,1]{2,1,0:T(8,128)S(1)} %get-tuple-element.704), channel_id=1, source_target_pairs={{1,0},{2,1},{3,2},{5,4},{6,5},{7,6},{9,8},{10,9},{11,10},{13,12},{... | collective-permute-start | bytes 656 | tf_op jit(solution)/shard_map/while/body/eval_jaxpr/ppermute | solution.py:23
  264.9 6.4 %collective-permute-start.3 = (f32[3,18,1]{2,1,0:T(8,128)S(1)}, f32[3,18,1]{2,1,0:T(8,128)S(1)}, u32[]{:S(2)}, u32[]{:S(2)}) collective-permute-start(f32[3,18,1]{2,1,0:T(8,128)S(1)} %get-tuple-element.705), channel_id=1, source_target_pairs={{0,1},{1,2},{2,3},{4,5},{5,6},{6,7},{8,9},{9,10},{10,11},{12,13},{... | collective-permute-start | bytes 656 | tf_op jit(solution)/shard_map/while/body/eval_jaxpr/ppermute | solution.py:20
  280.5 7.3 %collective-permute-start.2 = (f32[3,18,1]{2,1,0:T(8,128)S(1)}, f32[3,18,1]{2,1,0:T(8,128)S(1)}, u32[]{:S(2)}, u32[]{:S(2)}) collective-permute-start(f32[3,18,1]{2,1,0:T(8,128)S(1)} %get-tuple-element.704), channel_id=1, source_target_pairs={{1,0},{2,1},{3,2},{5,4},{6,5},{7,6},{9,8},{10,9},{11,10},{13,12},{... | collective-permute-start | bytes 656 | tf_op jit(solution)/shard_map/while/body/eval_jaxpr/ppermute | solution.py:23
  298.1 7.3 %collective-permute-start.2 = (f32[3,18,1]{2,1,0:T(8,128)S(1)}, f32[3,18,1]{2,1,0:T(8,128)S(1)}, u32[]{:S(2)}, u32[]{:S(2)}) collective-permute-start(f32[3,18,1]{2,1,0:T(8,128)S(1)} %get-tuple-element.704), channel_id=1, source_target_pairs={{1,0},{2,1},{3,2},{5,4},{6,5},{7,6},{9,8},{10,9},{11,10},{13,12},{... | collective-permute-start | bytes 656 | tf_op jit(solution)/shard_map/while/body/eval_jaxpr/ppermute | solution.py:23
  315.6 7.3 %collective-permute-start.2 = (f32[3,18,1]{2,1,0:T(8,128)S(1)}, f32[3,18,1]{2,1,0:T(8,128)S(1)}, u32[]{:S(2)}, u32[]{:S(2)}) collective-permute-start(f32[3,18,1]{2,1,0:T(8,128)S(1)} %get-tuple-element.704), channel_id=1, source_target_pairs={{1,0},{2,1},{3,2},{5,4},{6,5},{7,6},{9,8},{10,9},{11,10},{13,12},{... | collective-permute-start | bytes 656 | tf_op jit(solution)/shard_map/while/body/eval_jaxpr/ppermute | solution.py:23
  317.5 6.4 %collective-permute-start.3 = (f32[3,18,1]{2,1,0:T(8,128)S(1)}, f32[3,18,1]{2,1,0:T(8,128)S(1)}, u32[]{:S(2)}, u32[]{:S(2)}) collective-permute-start(f32[3,18,1]{2,1,0:T(8,128)S(1)} %get-tuple-element.705), channel_id=1, source_target_pairs={{0,1},{1,2},{2,3},{4,5},{5,6},{6,7},{8,9},{9,10},{10,11},{12,13},{... | collective-permute-start | bytes 656 | tf_op jit(solution)/shard_map/while/body/eval_jaxpr/ppermute | solution.py:20
  333.2 7.3 %collective-permute-start.2 = (f32[3,18,1]{2,1,0:T(8,128)S(1)}, f32[3,18,1]{2,1,0:T(8,128)S(1)}, u32[]{:S(2)}, u32[]{:S(2)}) collective-permute-start(f32[3,18,1]{2,1,0:T(8,128)S(1)} %get-tuple-element.704), channel_id=1, source_target_pairs={{1,0},{2,1},{3,2},{5,4},{6,5},{7,6},{9,8},{10,9},{11,10},{13,12},{... | collective-permute-start | bytes 656 | tf_op jit(solution)/shard_map/while/body/eval_jaxpr/ppermute | solution.py:23
  335.1 6.4 %collective-permute-start.3 = (f32[3,18,1]{2,1,0:T(8,128)S(1)}, f32[3,18,1]{2,1,0:T(8,128)S(1)}, u32[]{:S(2)}, u32[]{:S(2)}) collective-permute-start(f32[3,18,1]{2,1,0:T(8,128)S(1)} %get-tuple-element.705), channel_id=1, source_target_pairs={{0,1},{1,2},{2,3},{4,5},{5,6},{6,7},{8,9},{9,10},{10,11},{12,13},{... | collective-permute-start | bytes 656 | tf_op jit(solution)/shard_map/while/body/eval_jaxpr/ppermute | solution.py:20
  350.7 7.3 %collective-permute-start.2 = (f32[3,18,1]{2,1,0:T(8,128)S(1)}, f32[3,18,1]{2,1,0:T(8,128)S(1)}, u32[]{:S(2)}, u32[]{:S(2)}) collective-permute-start(f32[3,18,1]{2,1,0:T(8,128)S(1)} %get-tuple-element.704), channel_id=1, source_target_pairs={{1,0},{2,1},{3,2},{5,4},{6,5},{7,6},{9,8},{10,9},{11,10},{13,12},{... | collective-permute-start | bytes 656 | tf_op jit(solution)/shard_map/while/body/eval_jaxpr/ppermute | solution.py:23
  368.3 7.3 %collective-permute-start.2 = (f32[3,18,1]{2,1,0:T(8,128)S(1)}, f32[3,18,1]{2,1,0:T(8,128)S(1)}, u32[]{:S(2)}, u32[]{:S(2)}) collective-permute-start(f32[3,18,1]{2,1,0:T(8,128)S(1)} %get-tuple-element.704), channel_id=1, source_target_pairs={{1,0},{2,1},{3,2},{5,4},{6,5},{7,6},{9,8},{10,9},{11,10},{13,12},{... | collective-permute-start | bytes 656 | tf_op jit(solution)/shard_map/while/body/eval_jaxpr/ppermute | solution.py:23
  385.8 7.3 %collective-permute-start.2 = (f32[3,18,1]{2,1,0:T(8,128)S(1)}, f32[3,18,1]{2,1,0:T(8,128)S(1)}, u32[]{:S(2)}, u32[]{:S(2)}) collective-permute-start(f32[3,18,1]{2,1,0:T(8,128)S(1)} %get-tuple-element.704), channel_id=1, source_target_pairs={{1,0},{2,1},{3,2},{5,4},{6,5},{7,6},{9,8},{10,9},{11,10},{13,12},{... | collective-permute-start | bytes 656 | tf_op jit(solution)/shard_map/while/body/eval_jaxpr/ppermute | solution.py:23
  387.8 6.4 %collective-permute-start.3 = (f32[3,18,1]{2,1,0:T(8,128)S(1)}, f32[3,18,1]{2,1,0:T(8,128)S(1)}, u32[]{:S(2)}, u32[]{:S(2)}) collective-permute-start(f32[3,18,1]{2,1,0:T(8,128)S(1)} %get-tuple-element.705), channel_id=1, source_target_pairs={{0,1},{1,2},{2,3},{4,5},{5,6},{6,7},{8,9},{9,10},{10,11},{12,13},{... | collective-permute-start | bytes 656 | tf_op jit(solution)/shard_map/while/body/eval_jaxpr/ppermute | solution.py:20
  403.4 7.3 %collective-permute-start.2 = (f32[3,18,1]{2,1,0:T(8,128)S(1)}, f32[3,18,1]{2,1,0:T(8,128)S(1)}, u32[]{:S(2)}, u32[]{:S(2)}) collective-permute-start(f32[3,18,1]{2,1,0:T(8,128)S(1)} %get-tuple-element.704), channel_id=1, source_target_pairs={{1,0},{2,1},{3,2},{5,4},{6,5},{7,6},{9,8},{10,9},{11,10},{13,12},{... | collective-permute-start | bytes 656 | tf_op jit(solution)/shard_map/while/body/eval_jaxpr/ppermute | solution.py:23
  405.3 6.4 %collective-permute-start.3 = (f32[3,18,1]{2,1,0:T(8,128)S(1)}, f32[3,18,1]{2,1,0:T(8,128)S(1)}, u32[]{:S(2)}, u32[]{:S(2)}) collective-permute-start(f32[3,18,1]{2,1,0:T(8,128)S(1)} %get-tuple-element.705), channel_id=1, source_target_pairs={{0,1},{1,2},{2,3},{4,5},{5,6},{6,7},{8,9},{9,10},{10,11},{12,13},{... | collective-permute-start | bytes 656 | tf_op jit(solution)/shard_map/while/body/eval_jaxpr/ppermute | solution.py:20
  421.0 7.3 %collective-permute-start.2 = (f32[3,18,1]{2,1,0:T(8,128)S(1)}, f32[3,18,1]{2,1,0:T(8,128)S(1)}, u32[]{:S(2)}, u32[]{:S(2)}) collective-permute-start(f32[3,18,1]{2,1,0:T(8,128)S(1)} %get-tuple-element.704), channel_id=1, source_target_pairs={{1,0},{2,1},{3,2},{5,4},{6,5},{7,6},{9,8},{10,9},{11,10},{13,12},{... | collective-permute-start | bytes 656 | tf_op jit(solution)/shard_map/while/body/eval_jaxpr/ppermute | solution.py:23
  438.5 7.3 %collective-permute-start.2 = (f32[3,18,1]{2,1,0:T(8,128)S(1)}, f32[3,18,1]{2,1,0:T(8,128)S(1)}, u32[]{:S(2)}, u32[]{:S(2)}) collective-permute-start(f32[3,18,1]{2,1,0:T(8,128)S(1)} %get-tuple-element.704), channel_id=1, source_target_pairs={{1,0},{2,1},{3,2},{5,4},{6,5},{7,6},{9,8},{10,9},{11,10},{13,12},{... | collective-permute-start | bytes 656 | tf_op jit(solution)/shard_map/while/body/eval_jaxpr/ppermute | solution.py:23
  456.1 7.3 %collective-permute-start.2 = (f32[3,18,1]{2,1,0:T(8,128)S(1)}, f32[3,18,1]{2,1,0:T(8,128)S(1)}, u32[]{:S(2)}, u32[]{:S(2)}) collective-permute-start(f32[3,18,1]{2,1,0:T(8,128)S(1)} %get-tuple-element.704), channel_id=1, source_target_pairs={{1,0},{2,1},{3,2},{5,4},{6,5},{7,6},{9,8},{10,9},{11,10},{13,12},{... | collective-permute-start | bytes 656 | tf_op jit(solution)/shard_map/while/body/eval_jaxpr/ppermute | solution.py:23
  458.0 6.4 %collective-permute-start.3 = (f32[3,18,1]{2,1,0:T(8,128)S(1)}, f32[3,18,1]{2,1,0:T(8,128)S(1)}, u32[]{:S(2)}, u32[]{:S(2)}) collective-permute-start(f32[3,18,1]{2,1,0:T(8,128)S(1)} %get-tuple-element.705), channel_id=1, source_target_pairs={{0,1},{1,2},{2,3},{4,5},{5,6},{6,7},{8,9},{9,10},{10,11},{12,13},{... | collective-permute-start | bytes 656 | tf_op jit(solution)/shard_map/while/body/eval_jaxpr/ppermute | solution.py:20
  473.6 7.3 %collective-permute-start.2 = (f32[3,18,1]{2,1,0:T(8,128)S(1)}, f32[3,18,1]{2,1,0:T(8,128)S(1)}, u32[]{:S(2)}, u32[]{:S(2)}) collective-permute-start(f32[3,18,1]{2,1,0:T(8,128)S(1)} %get-tuple-element.704), channel_id=1, source_target_pairs={{1,0},{2,1},{3,2},{5,4},{6,5},{7,6},{9,8},{10,9},{11,10},{13,12},{... | collective-permute-start | bytes 656 | tf_op jit(solution)/shard_map/while/body/eval_jaxpr/ppermute | solution.py:23
  475.6 6.4 %collective-permute-start.3 = (f32[3,18,1]{2,1,0:T(8,128)S(1)}, f32[3,18,1]{2,1,0:T(8,128)S(1)}, u32[]{:S(2)}, u32[]{:S(2)}) collective-permute-start(f32[3,18,1]{2,1,0:T(8,128)S(1)} %get-tuple-element.705), channel_id=1, source_target_pairs={{0,1},{1,2},{2,3},{4,5},{5,6},{6,7},{8,9},{9,10},{10,11},{12,13},{... | collective-permute-start | bytes 656 | tf_op jit(solution)/shard_map/while/body/eval_jaxpr/ppermute | solution.py:20
  492.7 19.7 %collective-permute-start.6 = (f32[80,1,128]{0,1,2:T(1,128)}, f32[80,1,128]{0,1,2:T(1,128)}, u32[]{:S(2)}, u32[]{:S(2)}) collective-permute-start(f32[80,1,128]{0,1,2:T(1,128)} %slice.1001), channel_id=1, source_target_pairs={{0,4},{4,8},{8,12},{12,16},{16,20},{20,24},{24,28},{1,5},{5,9},{9,... | collective-permute-start | bytes 122888 | tf_op jit(solution)/shard_map/ppermute | solution.py:31
  495.5 8.2 %collective-permute-start.9 = (f32[80,16,1]{0,1,2:T(8,128)S(1)}, f32[80,16,1]{0,1,2:T(8,128)S(1)}, u32[]{:S(2)}, u32[]{:S(2)}) collective-permute-start(f32[80,16,1]{0,1,2:T(8,128)S(1)} %slice.1014), channel_id=1, source_target_pairs={{0,1},{1,2},{2,3},{4,5},{5,6},{6,7},{8,9},{9,10},{10,11},{12,13},{... | collective-permute-start | bytes 15368 | tf_op jit(solution)/shard_map/ppermute | solution.py:31
  527.0 13.8 %collective-permute-start.10 = (f32[2,80,22,3]{1,0,3,2:T(2,128)}, f32[2,80,22,3]{1,0,3,2:T(2,128)}, u32[]{:S(2)}, u32[]{:S(2)}) collective-permute-start(f32[2,80,22,3]{1,0,3,2:T(2,128)} %copy.388), channel_id=1, source_target_pairs={{0,1},{1,2},{2,3},{4,5},{5,6},{6,7},{8,9},{9,10},{10,11},{12,13},{... | collective-permute-start | bytes 126728 | tf_op jit(solution)/shard_map/ppermute | solution.py:20
  532.0 10.6 %collective-permute-start.11 = (f32[2,80,22,3]{1,0,3,2:T(2,128)}, f32[2,80,22,3]{1,0,3,2:T(2,128)}, u32[]{:S(2)}, u32[]{:S(2)}) collective-permute-start(f32[2,80,22,3]{1,0,3,2:T(2,128)} %copy.390), channel_id=1, source_target_pairs={{1,0},{2,1},{3,2},{5,4},{6,5},{7,6},{9,8},{10,9},{11,10},{13,12},{... | collective-permute-start | bytes 126728 | tf_op jit(solution)/shard_map/ppermute | solution.py:23
  (201 other events, 1636.7 us)
where the time goes:
time: 580 us; the launch traced here: 570 us
  starting transfers between devices  325 us (56%)
  other arithmetic  126 us (22%)
  waiting for transfers between devices  69.9 us (12%)
  local copies, waits for them, and re-layouts  44.2 us (8%)
    ppermute x50, starting transfers between devices, with_halo(): lax.ppermute(lax.slice_in_dim(block, block.shape[dim] - width, None, axis...  213 us
    ppermute x50, starting transfers between devices, with_halo(): lax.ppermute(lax.slice_in_dim(block, 0, width, axis=dim), axis, backward)  99.2 us
    ppermute x50, waiting for transfers between devices, with_halo(): lax.ppermute(lax.slice_in_dim(block, block.shape[dim] - width, None, axis...  69.7 us
    mul x34, other arithmetic, column_solve(): result[level] = values[level] + gains[level] * result[level + 1]  22.7 us
    add x24, other arithmetic, one_round(): east_total = east_total + crop(east_ext, margin)  20.2 us
    add x24, other arithmetic, one_round(): north_total = north_total + crop(north_ext, margin)  19.7 us
    ppermute x4, starting transfers between devices, from_behind(): lax.ppermute(value, axis, [(source, source + steps) for source in range(l...  12.8 us
  transfers between devices with their start and end apart: 104, of which 48 were waited for; matrix products, arithmetic and copies ran while one was open for 24% of the time, Pallas kernels for 0%

commit v1 on v0

v1 whole, which is shorter than its diff:
```python
import functools

import jax
import jax.numpy as jnp
from jax import lax
from jax.experimental import pallas as pl
from jax.experimental.pallas import tpu as pltpu
from jax.sharding import PartitionSpec as P

K = 80
STEPS = 24
CX = 16
CY = 128
GROUP = 8
GROUPS = K // GROUP
CHUNKS = 5
CHUNK = GROUPS // CHUNKS
ROWS = 72
OWN = 32
EAST_ROWS = 7 * GROUP
WEST_ROWS = 6 * GROUP
MESH = pl.DeviceIdType.MESH

DIRECTIONS = [(dx, dy) for dx in (1, -1, 2, -2, 0) for dy in (0, 1, -1) if (dx, dy) != (0, 0)]


def roll(x, shift, axis):
    return pltpu.roll(x, shift % x.shape[axis], axis)


def kernel(
    nx, ny,
    tracers, velocity, mixing, levels, surface, transport, forcing,
    surface_out, transport_out, mean_out, tracers_out,
    fields, pack_w, pack_e, halo_e, halo_w, lev,
    text, velx, vely, mix, gain, lower, inverse, values,
    east_send, west_send, east_recv, west_recv,
    north_send, south_send, north_recv, south_recv,
    coef, state,
    local_sem, out_sem, b_send, b_recv, x_send, x_recv, y_send, y_recv,
):
    gx = lax.axis_index("gx")
    gy = lax.axis_index("gy")

    def has(dx, dy):
        x, y = gx + dx, gy + dy
        return (x >= 0) & (x < nx) & (y >= 0) & (y < ny)

    def device(dx, dy):
        return (lax.rem(gx + dx + nx, nx), lax.rem(gy + dy + ny, ny))

    own = pl.ds(OWN, CX)
    loads = [
        pltpu.make_async_copy(surface, fields.at[0, own, :], local_sem.at[0]),
        pltpu.make_async_copy(transport, fields.at[1:3, own, :], local_sem.at[1]),
        pltpu.make_async_copy(forcing, fields.at[3:5, own, :], local_sem.at[2]),
        pltpu.make_async_copy(levels, lev, local_sem.at[3]),
        pltpu.make_async_copy(tracers, text.at[:, :, 8:24, :], local_sem.at[4]),
        pltpu.make_async_copy(velocity.at[0], velx.at[:, 8:24, :], local_sem.at[5]),
        pltpu.make_async_copy(velocity.at[1], vely, local_sem.at[6]),
        pltpu.make_async_copy(mixing, mix.at[0 : K - 1], local_sem.at[7]),
    ]
    for load in loads:
        load.start()

    barrier = pltpu.get_barrier_semaphore()
    count = jnp.int32(0)
    for dx, dy in DIRECTIONS:
        there = has(dx, dy)

        @pl.when(there)
        def _():
            pl.semaphore_signal(barrier, inc=1, device_id=device(dx, dy), device_id_type=MESH)

        count = count + there.astype(jnp.int32)

    lane = lax.broadcasted_iota(jnp.int32, (CX, CY), 1)

    for load in loads[:4]:
        load.wait()
    fields[5, OWN : OWN + CX, :] = lev[...].astype(jnp.float32) * (1.0 / K)
    for group in range(2):
        east = None
        west = None
        for slot in range(4 if group == 0 else 2):
            x = fields[4 * group + slot, OWN : OWN + CX, :]
            inside = (lane >= 32 * slot) & (lane < 32 * slot + 32)
            to_east = roll(x, 32 * slot + 32, 1)
            to_west = roll(x, 32 * slot, 1)
            east = to_east if east is None else jnp.where(inside, to_east, east)
            west = to_west if west is None else jnp.where(inside, to_west, west)
        pack_e[group] = east
        pack_w[group] = west

    def barotropic_copy(index):
        dx, dy = DIRECTIONS[index]
        rows = 8 if dx == -2 else CX
        start = CX * (2 - dx)
        if dy == 0:
            src, dst = fields.at[:, pl.ds(OWN, rows), :], fields
        elif dy == 1:
            src, dst = pack_e.at[:, pl.ds(0, rows), :], halo_w
        else:
            src, dst = pack_w.at[:, pl.ds(0, rows), :], halo_e
        return (
            pltpu.make_async_remote_copy(
                src_ref=src,
                dst_ref=dst.at[:, pl.ds(start, rows), :],
                send_sem=b_send.at[index],
                recv_sem=b_recv.at[index],
                device_id=device(dx, dy),
                device_id_type=MESH,
            ),
            dst,
            start,
            rows,
        )

    def x_copy(direction, chunk):
        src, dst, dx = ((east_send, east_recv, 1), (west_send, west_recv, -1))[direction]
        part = pl.ds(chunk * CHUNK, CHUNK)
        return pltpu.make_async_remote_copy(
            src_ref=src.at[part], dst_ref=dst.at[part],
            send_sem=x_send.at[direction, chunk], recv_sem=x_recv.at[direction, chunk],
            device_id=device(dx, 0), device_id_type=MESH,
        ), dst, part, dx

    def y_copy(direction):
        src, dst, dy = ((north_send, north_recv, 1), (south_send, south_recv, -1))[direction]
        return pltpu.make_async_remote_copy(
            src_ref=src, dst_ref=dst,
            send_sem=y_send.at[direction], recv_sem=y_recv.at[direction],
            device_id=device(0, dy), device_id_type=MESH,
        ), dst, dy

    pl.semaphore_wait(barrier, count)
    for index, (dx, dy) in enumerate(DIRECTIONS):
        copy, dst, start, rows = barotropic_copy(index)
        pl.when(has(dx, dy))(copy.start)

        @pl.when(jnp.logical_not(has(-dx, -dy)))
        def _():
            dst[:, pl.ds(start, rows), :] = jnp.zeros((dst.shape[0], rows, CY), jnp.float32)

    for load in loads[4:7]:
        load.wait()

    def pack_x(g, carry):
        for l in range(GROUP):
            k = g * GROUP + l
            for t in range(2):
                east_send[g, 7 * l + 3 * t : 7 * l + 3 * t + 3, :] = text[t, k, 21:24, :]
                west_send[g, 6 * l + 3 * t : 6 * l + 3 * t + 3, :] = text[t, k, 8:11, :]
            east_send[g, 7 * l + 6 : 7 * l + 7, :] = velx[k, 23:24, :]
        return carry

    for chunk in range(CHUNKS):
        lax.fori_loop(chunk * CHUNK, chunk * CHUNK + CHUNK, pack_x, 0)
        for direction in range(2):
            copy, dst, part, dx = x_copy(direction, chunk)
            pl.when(has(dx, 0))(copy.start)

            @pl.when(jnp.logical_not(has(-dx, 0)))
            def _():
                dst[part] = jnp.zeros((CHUNK,) + dst.shape[1:], jnp.float32)

    def pack_y(g, carry):
        north = jnp.zeros((CX, CY), jnp.float32)
        south = jnp.zeros((CX, CY), jnp.float32)
        for l in range(GROUP):
            k = g * GROUP + l
            t0 = text[0, k, 8:24, :]
            t1 = text[1, k, 8:24, :]
            high = jnp.where(
                lane >= 125, t0,
                jnp.where(lane >= 122, roll(t1, -3, 1), jnp.where(lane == 121, roll(vely[k], -6, 1), 0.0)),
            )
            low = jnp.where(lane < 3, t0, jnp.where(lane < 6, roll(t1, 3, 1), 0.0))
            north = north + roll(high, 16 * l + 8, 1)
            south = south + roll(low, 16 * l, 1)
        north_send[g] = north
        south_send[g] = south
        return carry

    lax.fori_loop(0, GROUPS, pack_y, 0)
    for direction in range(2):
        copy, dst, dy = y_copy(direction)
        pl.when(has(0, dy))(copy.start)

        @pl.when(jnp.logical_not(has(0, -dy)))
        def _():
            dst[...] = jnp.zeros(dst.shape, jnp.float32)

    loads[7].wait()
    mix[K - 1] = jnp.zeros((CX, CY), jnp.float32)

    def factor(k, carry):
        below, previous = carry
        upper = jnp.where(k + 1 < lev[...], mix[k], 0.0)
        inv = 1.0 / (1.0 + below + upper - below * previous)
        g = upper * inv
        gain[k] = g
        inverse[k] = inv
        lower[k] = below * inv
        return upper, g

    zero = jnp.zeros((CX, CY), jnp.float32)
    lax.fori_loop(0, K, factor, (zero, zero), unroll=4)

    for index, (dx, dy) in enumerate(DIRECTIONS):
        copy = barotropic_copy(index)[0]
        pl.when(has(-dx, -dy))(copy.wait_recv)

    wide = lax.broadcasted_iota(jnp.int32, (ROWS, CY), 1)

    def beside(index):
        group, slot = divmod(index, 4)
        return jnp.where(
            wide < 64, roll(halo_e[group], -32 * slot, 1), roll(halo_w[group], 96 - 32 * slot, 1)
        )

    def upper_x(pair):
        return tuple(roll(x, -1, 0) for x in pair)

    def lower_x(pair):
        return tuple(roll(x, 1, 0) for x in pair)

    def upper_y(pair):
        a, b = (roll(x, -1, 1) for x in pair)
        return jnp.where(wide == CY - 1, b, a), jnp.where(wide == CY - 1, a, b)

    def lower_y(pair):
        a, b = (roll(x, 1, 1) for x in pair)
        return jnp.where(wide == 0, b, a), jnp.where(wide == 0, a, b)

    depth = (fields[5], beside(5))
    east_depth = tuple(jnp.minimum(a, b) for a, b in zip(depth, upper_x(depth)))
    north_depth = tuple(jnp.minimum(a, b) for a, b in zip(depth, upper_y(depth)))
    for tile in range(2):
        other = (lambda i: fields[i]) if tile == 0 else beside
        coef[0, tile] = 0.9 * east_depth[tile]
        coef[1, tile] = 0.5 * east_depth[tile] * other(3)
        coef[2, tile] = 0.9 * north_depth[tile]
        coef[3, tile] = 0.5 * north_depth[tile] * other(4)
        coef[4, tile] = east_depth[tile]
        coef[5, tile] = north_depth[tile]
        state[0, tile] = other(0)
        state[1, tile] = jnp.where(east_depth[tile] > 0.0, other(1), 0.0)
        state[2, tile] = jnp.where(north_depth[tile] > 0.0, other(2), 0.0)
        state[3, tile] = jnp.zeros((ROWS, CY), jnp.float32)
        state[4, tile] = jnp.zeros((ROWS, CY), jnp.float32)

    def substep(step, carry):
        east = (state[1, 0], state[1, 1])
        north = (state[2, 0], state[2, 1])
        east_low = lower_x(east)
        north_low = lower_y(north)
        height = tuple(
            state[0, i] - 0.5 * ((east[i] - east_low[i]) + (north[i] - north_low[i])) for i in range(2)
        )
        high_x = upper_x(height)
        high_y = upper_y(height)
        for i in range(2):
            state[0, i] = height[i]
            e = east[i] - coef[0, i] * (high_x[i] - height[i]) + coef[1, i]
            n = north[i] - coef[2, i] * (high_y[i] - height[i]) + coef[3, i]
            state[1, i] = e
            state[2, i] = n
            state[3, i] = state[3, i] + e
            state[4, i] = state[4, i] + n
        return carry

    lax.fori_loop(0, STEPS, substep, 0)

    surface_out[...] = state[0, 0, OWN : OWN + CX, :]
    transport_out[0] = state[1, 0, OWN : OWN + CX, :]
    transport_out[1] = state[2, 0, OWN : OWN + CX, :]
    mean_out[0] = state[3, 0, OWN : OWN + CX, :] * (1.0 / STEPS)
    mean_out[1] = state[4, 0, OWN : OWN + CX, :] * (1.0 / STEPS)

    scale = 0.01 / STEPS
    for i in range(2):
        state[3, i] = scale * state[3, i] / jnp.maximum(coef[4, i], 1.0 / K)
        state[4, i] = scale * state[4, i] / jnp.maximum(coef[5, i], 1.0 / K)

    here = slice(OWN, OWN + CX)
    behind = slice(OWN - 1, OWN + CX - 1)
    east_speed, west_speed = state[3, 0, here, :], state[3, 0, behind, :]
    east_limit, west_limit = coef[4, 0, here, :], coef[4, 0, behind, :]
    north_speed, north_limit = state[4, 0, here, :], coef[5, 0, here, :]
    south_speed = jnp.where(lane == 0, roll(state[4, 1, here, :], 1, 1), roll(north_speed, 1, 1))
    south_limit = jnp.where(lane == 0, roll(coef[5, 1, here, :], 1, 1), roll(north_limit, 1, 1))

    for direction in range(2):
        copy, dst, dy = y_copy(direction)
        pl.when(has(0, -dy))(copy.wait_recv)

    def flux(cells, w, size):
        a, b, c, d, e, f = cells
        even = (a + f) - 8.0 * (b + e) + 37.0 * (c + d)
        odd = (a - f) - 5.0 * (b - e) + 10.0 * (c - d)
        return w * even + size * odd

    def face(mid, limit, value):
        w = jnp.where(mid < limit, value, 0.0) * (1.0 / 60.0)
        return w, jnp.abs(w)

    def advance(g, carry):
        carry = list(carry)
        packed_low = north_recv[g]
        packed_high = south_recv[g]
        for l in range(GROUP):
            k = g * GROUP + l
            mid = (k.astype(jnp.float32) + 0.5) * (1.0 / K)
            velx[k, 7:8, :] = east_recv[g, 7 * l + 6 : 7 * l + 7, :]
            low = roll(packed_low, 120 - 16 * l, 1)
            high = roll(packed_high, -16 * l, 1)
            vy = vely[k]
            we, ae = face(mid, east_limit, velx[k, 8:24, :] + east_speed)
            ww, aw = face(mid, west_limit, velx[k, 7:23, :] + west_speed)
            wn, an = face(mid, north_limit, vy + north_speed)
            ws, as_ = face(
                mid, south_limit, jnp.where(lane == 0, roll(low, 7, 1), roll(vy, 1, 1)) + south_speed
            )
            inv = inverse[k]
            low_gain = lower[k]
            for t in range(2):
                text[t, k, 5:8, :] = east_recv[g, 7 * l + 3 * t : 7 * l + 3 * t + 3, :]
                text[t, k, 24:27, :] = west_recv[g, 6 * l + 3 * t : 6 * l + 3 * t + 3, :]
                cells = [text[t, k, 8 + s : 24 + s, :] for s in range(-3, 4)]
                center = cells[3]
                change = flux(cells[1:], we, ae) - flux(cells[:6], ww, aw)
                below = low if t == 0 else roll(low, 3, 1)
                above = high if t == 0 else roll(high, -3, 1)
                cells = (
                    [roll(jnp.where(lane >= CY - s, below, center), s, 1) for s in (3, 2, 1)]
                    + [center]
                    + [roll(jnp.where(lane < s, above, center), -s, 1) for s in (1, 2, 3)]
                )
                change = change + (flux(cells[1:], wn, an) - flux(cells[:6], ws, as_))
                carry[t] = (center - change) * inv + low_gain * carry[t]
                values[t, k] = carry[t]
        return tuple(carry)

    carry = (zero, zero)
    for chunk in range(CHUNKS):
        for direction in range(2):
            copy, dst, part, dx = x_copy(direction, chunk)
            pl.when(has(-dx, 0))(copy.wait_recv)
        carry = lax.fori_loop(chunk * CHUNK, chunk * CHUNK + CHUNK, advance, carry)

    def out_copy(chunk):
        part = pl.ds(chunk * CHUNK * GROUP, CHUNK * GROUP)
        return pltpu.make_async_copy(values.at[:, part], tracers_out.at[:, part], out_sem.at[chunk])

    def back(index, carry):
        k = K - 1 - index
        g = gain[k]
        result = tuple(values[t, k] + g * carry[t] for t in range(2))
        for t in range(2):
            values[t, k] = result[t]
        return result

    carry = (zero, zero)
    for chunk in range(CHUNKS - 1, -1, -1):
        first = (CHUNKS - 1 - chunk) * CHUNK * GROUP
        carry = lax.fori_loop(first, first + CHUNK * GROUP, back, carry, unroll=4)
        out_copy(chunk).start()
    for chunk in range(CHUNKS):
        out_copy(chunk).wait()

    for index, (dx, dy) in enumerate(DIRECTIONS):
        pl.when(has(dx, dy))(barotropic_copy(index)[0].wait_send)
    for direction in range(2):
        copy, _, dy = y_copy(direction)
        pl.when(has(0, dy))(copy.wait_send)
        for chunk in range(CHUNKS):
            copy, _, _, dx = x_copy(direction, chunk)
            pl.when(has(dx, 0))(copy.wait_send)


def per_device(nx, ny, tracers, velocity, mixing, levels, surface, transport, forcing):
    f32 = jnp.float32
    anywhere = pl.BlockSpec(memory_space=pl.ANY)
    vmem = pl.BlockSpec(memory_space=pltpu.VMEM)
    return pl.pallas_call(
        functools.partial(kernel, nx, ny),
        out_shape=(
            jax.ShapeDtypeStruct((CX, CY), f32),
            jax.ShapeDtypeStruct((2, CX, CY), f32),
            jax.ShapeDtypeStruct((2, CX, CY), f32),
            jax.ShapeDtypeStruct((2, K, CX, CY), f32),
        ),
        in_specs=[anywhere] * 7,
        out_specs=(vmem, vmem, vmem, anywhere),
        scratch_shapes=[
            pltpu.VMEM((6, ROWS, CY), f32),
            pltpu.VMEM((2, CX, CY), f32),
            pltpu.VMEM((2, CX, CY), f32),
            pltpu.VMEM((2, ROWS, CY), f32),
            pltpu.VMEM((2, ROWS, CY), f32),
            pltpu.VMEM((CX, CY), jnp.int32),
            pltpu.VMEM((2, K, 32, CY), f32),
            pltpu.VMEM((K, 24, CY), f32),
            pltpu.VMEM((K, CX, CY), f32),
            pltpu.VMEM((K, CX, CY), f32),
            pltpu.VMEM((K, CX, CY), f32),
            pltpu.VMEM((K, CX, CY), f32),
            pltpu.VMEM((K, CX, CY), f32),
            pltpu.VMEM((2, K, CX, CY), f32),
            pltpu.VMEM((GROUPS, EAST_ROWS, CY), f32),
            pltpu.VMEM((GROUPS, WEST_ROWS, CY), f32),
            pltpu.VMEM((GROUPS, EAST_ROWS, CY), f32),
            pltpu.VMEM((GROUPS, WEST_ROWS, CY), f32),
            pltpu.VMEM((GROUPS, CX, CY), f32),
            pltpu.VMEM((GROUPS, CX, CY), f32),
            pltpu.VMEM((GROUPS, CX, CY), f32),
            pltpu.VMEM((GROUPS, CX, CY), f32),
            pltpu.VMEM((6, 2, ROWS, CY), f32),
            pltpu.VMEM((5, 2, ROWS, CY), f32),
            pltpu.SemaphoreType.DMA((8,)),
            pltpu.SemaphoreType.DMA((CHUNKS,)),
            pltpu.SemaphoreType.DMA((len(DIRECTIONS),)),
            pltpu.SemaphoreType.DMA((len(DIRECTIONS),)),
            pltpu.SemaphoreType.DMA((2, CHUNKS)),
            pltpu.SemaphoreType.DMA((2, CHUNKS)),
            pltpu.SemaphoreType.DMA((2,)),
            pltpu.SemaphoreType.DMA((2,)),
        ],
        compiler_params=pltpu.CompilerParams(
            collective_id=0, has_side_effects=True, vmem_limit_bytes=40 * 1024 * 1024
        ),
    )(tracers, velocity, mixing, levels, surface, transport, forcing)


def solution(mesh):
    placed = (
        P(None, None, "gx", "gy"),
        P(None, None, "gx", "gy"),
        P(None, "gx", "gy"),
        P("gx", "gy"),
        P("gx", "gy"),
        P(None, "gx", "gy"),
        P(None, "gx", "gy"),
    )
    return jax.shard_map(
        functools.partial(per_device, mesh.shape["gx"], mesh.shape["gy"]),
        mesh=mesh,
        in_specs=placed,
        out_specs=(
            P("gx", "gy"),
            P(None, "gx", "gy"),
            P(None, "gx", "gy"),
            P(None, None, "gx", "gy"),
        ),
        check_vma=False,
    )
```

time: 580 us -> 39.5 us (0.07); the launches traced: 570 us -> 39.1 us
  starting transfers between devices: 325 us -> 0 us
  other arithmetic: 126 us -> 0 us
  waiting for transfers between devices: 69.9 us -> 0 us
  local copies, waits for them, and re-layouts: 44.2 us -> 9.4 us
  Pallas kernels: 0 us -> 29 us
    ppermute x104 -> x0, starting transfers between devices: 325 us -> none  [the longest x50 213 us: with_halo(): lax.ppermute(lax.slice_in_dim(block, block.shape[dim] - width, None, axis...]
    ppermute x104 -> x0, waiting for transfers between devices: 69.9 us -> none  [the longest x50 69.7 us: with_halo(): lax.ppermute(lax.slice_in_dim(block, block.shape[dim] - width, None, axis...]
    add x49 -> x0, other arithmetic: 40 us -> none  [the longest x24 20.2 us: one_round(): east_total = east_total + crop(east_ext, margin)]
    mul x39 -> x0, other arithmetic: 36.4 us -> none  [the longest x34 22.7 us: column_solve(): result[level] = values[level] + gains[level] * result[level + 1]]
    pallas_call x0 -> x1, Pallas kernels: none -> 29 us  [per_device(): pl.pallas_call(functools.partial(kernel, nx, ny), out_shape=(jax.ShapeDty...]
    concatenate x54 -> x0, other arithmetic: 17.3 us -> none  [the longest x50 8.58 us: with_halo(): block = jnp.concatenate([low, block, high], axis=dim)]
    slice x58 -> x0, local copies, waits for them, and re-layouts: 15.7 us -> none  [the longest x27 8.16 us: with_halo(): lax.slice_in_dim(block, block.shape[dim] - width, None, axis=dim)]
    sub x32 -> x0, other arithmetic: 12 us -> none  [the longest x7 9.54 us: column_solve(): pivot = 1.0 + lower + upper - lower * gains[-1]]
  transfers between devices with their start and end apart: 104 -> 0, of which waited for: 48 -> 0; matrix products, arithmetic and copies ran while one was open for 24% -> 0% of each run, Pallas kernels for 0% -> 0%
where the time goes in v1:
time: 39.5 us; the launch traced here: 39.1 us
  Pallas kernels  29 us (73%)
  local copies, waits for them, and re-layouts  9.4 us (24%)
  between operations  0.66 us (2%)
    pallas_call x1, Pallas kernels, per_device(): pl.pallas_call(functools.partial(kernel, nx, ny), out_shape=(jax.ShapeDty...  29 us
    unnamed x18, local copies, waits for them, and re-layouts  9.4 us

profile of v1, /device:TPU:9, one launch (start us, length us, event | category | flops | bytes accessed | tf_op | source)
XLA Modules:
  0.0 39.1 jit_solution(14149891531181171909)
XLA Ops:
  0.6 0.0 copy-start
  0.6 1.3 %copy-done = f32[2,80,16,128]{3,2,1,0:T(8,128)S(1)} copy-done((f32[2,80,16,128]{3,2,1,0:T(8,128)S(1)}, f32[2,80,16,128]{3,2,1,0:T(8,128)}, u32[]{:S(2)}) %copy-start) | copy-done | bytes 1310744
  2.0 0.0 copy-start.1
  2.0 1.3 %copy-done.1 = f32[2,80,16,128]{3,2,1,0:T(8,128)S(1)} copy-done((f32[2,80,16,128]{3,2,1,0:T(8,128)S(1)}, f32[2,80,16,128]{3,2,1,0:T(8,128)}, u32[]{:S(2)}) %copy-start.1) | copy-done | bytes 1310744
  3.3 0.0 copy-start.2
  3.3 1.1 %copy-done.2 = f32[79,16,128]{2,1,0:T(8,128)S(1)} copy-done((f32[79,16,128]{2,1,0:T(8,128)S(1)}, f32[79,16,128]{2,1,0:T(8,128)}, u32[]{:S(2)}) %copy-start.2) | copy-done | bytes 647192
  4.4 0.0 copy-start.3
  4.4 0.7 %copy-done.3 = f32[2,16,128]{2,1,0:T(8,128)S(1)} copy-done((f32[2,16,128]{2,1,0:T(8,128)S(1)}, f32[2,16,128]{2,1,0:T(8,128)}, u32[]{:S(2)}) %copy-start.3) | copy-done | bytes 16408
  5.1 0.0 copy-start.4
  5.1 0.7 %copy-done.4 = f32[2,16,128]{2,1,0:T(8,128)S(1)} copy-done((f32[2,16,128]{2,1,0:T(8,128)S(1)}, f32[2,16,128]{2,1,0:T(8,128)}, u32[]{:S(2)}) %copy-start.4) | copy-done | bytes 16408
  5.8 0.0 copy-start.5
  5.8 0.7 %copy-done.5 = s32[16,128]{1,0:T(8,128)S(1)} copy-done((s32[16,128]{1,0:T(8,128)S(1)}, s32[16,128]{1,0:T(8,128)}, u32[]{:S(2)}) %copy-start.5) | copy-done | bytes 8216
  6.5 0.0 copy-start.6
  6.5 0.7 %copy-done.6 = f32[16,128]{1,0:T(8,128)S(1)} copy-done((f32[16,128]{1,0:T(8,128)S(1)}, f32[16,128]{1,0:T(8,128)}, u32[]{:S(2)}) %copy-start.6) | copy-done | bytes 8216
  7.2 29.0 %shard_map.102 = (f32[16,128]{1,0:T(8,128)S(1)}, f32[2,16,128]{2,1,0:T(8,128)S(1)}, f32[2,16,128]{2,1,0:T(8,128)S(1)}, f32[2,80,16,128]{3,2,1,0:T(8,128)S(1)}) custom-call(f32[2,80,16,128]{3,2,1,0:T(8,128)S(1)} %copy-done, f32[2,80,16,128]{3,2,1,0:T(8,128)S(1)} %copy-done.1, f32[79,16,128]{2,1,0:T(8,128)S(1)} %copy-done.2, s32[16,128]{1,0:T(8,128)S(1)} %copy-done.5, ...), custom_call_target="tpu_custom_call" | custom-call | tf_op jit(solution)/shard_map/pallas_call | solution.py:386
  36.2 0.6 %copy.15 = f32[16,128]{1,0:T(8,128)} copy(f32[16,128]{1,0:T(8,128)S(1)} %get-tuple-element.8) | data formatting | bytes 16384
  36.8 0.6 %copy.16 = f32[2,16,128]{2,1,0:T(8,128)} copy(f32[2,16,128]{2,1,0:T(8,128)S(1)} %get-tuple-element.9) | data formatting | bytes 32768
  37.4 0.6 %copy.17 = f32[2,16,128]{2,1,0:T(8,128)} copy(f32[2,16,128]{2,1,0:T(8,128)S(1)} %get-tuple-element.10) | data formatting | bytes 32768
  38.0 1.1 %copy.18 = f32[2,80,16,128]{3,2,1,0:T(8,128)} copy(f32[2,80,16,128]{3,2,1,0:T(8,128)S(1)} %get-tuple-element.11) | data formatting | bytes 2621440
Async XLA Ops:
  0.6 1.3 %copy-start = (f32[2,80,16,128]{3,2,1,0:T(8,128)S(1)}, f32[2,80,16,128]{3,2,1,0:T(8,128)}, u32[]{:S(2)}) copy-start(f32[2,80,16,128]{3,2,1,0:T(8,128)} %tracers.1) | copy-start | bytes 3932164
  2.0 1.3 %copy-start.1 = (f32[2,80,16,128]{3,2,1,0:T(8,128)S(1)}, f32[2,80,16,128]{3,2,1,0:T(8,128)}, u32[]{:S(2)}) copy-start(f32[2,80,16,128]{3,2,1,0:T(8,128)} %velocity.1) | copy-start | bytes 3932164
  3.3 1.1 %copy-start.2 = (f32[79,16,128]{2,1,0:T(8,128)S(1)}, f32[79,16,128]{2,1,0:T(8,128)}, u32[]{:S(2)}) copy-start(f32[79,16,128]{2,1,0:T(8,128)} %mixing.1) | copy-start | bytes 1941508
  4.4 0.7 %copy-start.3 = (f32[2,16,128]{2,1,0:T(8,128)S(1)}, f32[2,16,128]{2,1,0:T(8,128)}, u32[]{:S(2)}) copy-start(f32[2,16,128]{2,1,0:T(8,128)} %transport.1) | copy-start | bytes 49156
  5.1 0.7 %copy-start.4 = (f32[2,16,128]{2,1,0:T(8,128)S(1)}, f32[2,16,128]{2,1,0:T(8,128)}, u32[]{:S(2)}) copy-start(f32[2,16,128]{2,1,0:T(8,128)} %forcing.1) | copy-start | bytes 49156
  5.8 0.7 %copy-start.5 = (s32[16,128]{1,0:T(8,128)S(1)}, s32[16,128]{1,0:T(8,128)}, u32[]{:S(2)}) copy-start(s32[16,128]{1,0:T(8,128)} %levels.1) | copy-start | bytes 24580
  6.5 0.7 %copy-start.6 = (f32[16,128]{1,0:T(8,128)S(1)}, f32[16,128]{1,0:T(8,128)}, u32[]{:S(2)}) copy-start(f32[16,128]{1,0:T(8,128)} %surface.1) | copy-start | bytes 24580

commit v2 on v1

--- a/solution.py
+++ b/solution.py
@@ -16,6 +16,7 @@
 CHUNKS = 5
 CHUNK = GROUPS // CHUNKS
 ROWS = 72
+VMEM = 60 * 1024 * 1024
 OWN = 32
 EAST_ROWS = 7 * GROUP
 WEST_ROWS = 6 * GROUP
@@ -31,9 +32,9 @@
 def kernel(
     nx, ny,
     tracers, velocity, mixing, levels, surface, transport, forcing,
-    surface_out, transport_out, mean_out, tracers_out,
+    surface_out, transport_out, mean_out, values_out, gain_out,
     fields, pack_w, pack_e, halo_e, halo_w, lev,
-    text, velx, vely, mix, gain, lower, inverse, values,
+    text, velx, vely, mix, lower, inverse, values, gain, mean,
     east_send, west_send, east_recv, west_recv,
     north_send, south_send, north_recv, south_recv,
     coef, state,
@@ -206,6 +207,14 @@
 
     zero = jnp.zeros((CX, CY), jnp.float32)
     lax.fori_loop(0, K, factor, (zero, zero), unroll=4)
+    own_state = pl.ds(OWN, CX)
+    stores = [
+        pltpu.make_async_copy(gain, gain_out, out_sem.at[CHUNKS]),
+        pltpu.make_async_copy(state.at[0, 0, own_state, :], surface_out, out_sem.at[CHUNKS + 1]),
+        pltpu.make_async_copy(state.at[1:3, 0, own_state, :], transport_out, out_sem.at[CHUNKS + 2]),
+        pltpu.make_async_copy(mean, mean_out, out_sem.at[CHUNKS + 3]),
+    ]
+    stores[0].start()
 
     for index, (dx, dy) in enumerate(DIRECTIONS):
         copy = barotropic_copy(index)[0]
@@ -272,11 +281,10 @@
 
     lax.fori_loop(0, STEPS, substep, 0)
 
-    surface_out[...] = state[0, 0, OWN : OWN + CX, :]
-    transport_out[0] = state[1, 0, OWN : OWN + CX, :]
-    transport_out[1] = state[2, 0, OWN : OWN + CX, :]
-    mean_out[0] = state[3, 0, OWN : OWN + CX, :] * (1.0 / STEPS)
-    mean_out[1] = state[4, 0, OWN : OWN + CX, :] * (1.0 / STEPS)
+    mean[0] = state[3, 0, OWN : OWN + CX, :] * (1.0 / STEPS)
+    mean[1] = state[4, 0, OWN : OWN + CX, :] * (1.0 / STEPS)
+    for store in stores[1:]:
+        store.start()
 
     scale = 0.01 / STEPS
     for i in range(2):
@@ -348,26 +356,12 @@
             copy, dst, part, dx = x_copy(direction, chunk)
             pl.when(has(-dx, 0))(copy.wait_recv)
         carry = lax.fori_loop(chunk * CHUNK, chunk * CHUNK + CHUNK, advance, carry)
-
-    def out_copy(chunk):
         part = pl.ds(chunk * CHUNK * GROUP, CHUNK * GROUP)
-        return pltpu.make_async_copy(values.at[:, part], tracers_out.at[:, part], out_sem.at[chunk])
-
-    def back(index, carry):
-        k = K - 1 - index
-        g = gain[k]
-        result = tuple(values[t, k] + g * carry[t] for t in range(2))
-        for t in range(2):
-            values[t, k] = result[t]
-        return result
-
-    carry = (zero, zero)
-    for chunk in range(CHUNKS - 1, -1, -1):
-        first = (CHUNKS - 1 - chunk) * CHUNK * GROUP
-        carry = lax.fori_loop(first, first + CHUNK * GROUP, back, carry, unroll=4)
-        out_copy(chunk).start()
-    for chunk in range(CHUNKS):
-        out_copy(chunk).wait()
+        store = pltpu.make_async_copy(values.at[:, part], values_out.at[:, part], out_sem.at[chunk])
+        store.start()
+        stores.append(store)
+    for store in stores:
+        store.wait()
 
     for index, (dx, dy) in enumerate(DIRECTIONS):
         pl.when(has(dx, dy))(barotropic_copy(index)[0].wait_send)
@@ -379,20 +373,72 @@
             pl.when(has(dx, 0))(copy.wait_send)
 
 
+def finish(
+    surface, transport, mean, values, gain,
+    surface_out, transport_out, mean_out, tracers_out,
+    held, factor, result, small_sem, in_sem, out_sem,
+):
+    def part(chunk):
+        return pl.ds(chunk * CHUNK * GROUP, CHUNK * GROUP)
+
+    def loads(chunk):
+        return (
+            pltpu.make_async_copy(gain.at[part(chunk)], factor.at[part(chunk)], in_sem.at[0, chunk]),
+            pltpu.make_async_copy(values.at[:, part(chunk)], held.at[:, part(chunk)], in_sem.at[1, chunk]),
+        )
+
+    def out_copy(chunk):
+        return pltpu.make_async_copy(
+            result.at[:, part(chunk)], tracers_out.at[:, part(chunk)], out_sem.at[chunk]
+        )
+
+    for chunk in range(CHUNKS - 1, -1, -1):
+        for load in loads(chunk):
+            load.start()
+    small = [
+        pltpu.make_async_copy(surface, surface_out, small_sem.at[0]),
+        pltpu.make_async_copy(transport, transport_out, small_sem.at[1]),
+        pltpu.make_async_copy(mean, mean_out, small_sem.at[2]),
+    ]
+    for copy in small:
+        copy.start()
+
+    def back(index, carry):
+        k = K - 1 - index
+        g = factor[k]
+        now = tuple(held[t, k] + g * carry[t] for t in range(2))
+        for t in range(2):
+            result[t, k] = now[t]
+        return now
+
+    zero = jnp.zeros((CX, CY), jnp.float32)
+    carry = (zero, zero)
+    for chunk in range(CHUNKS - 1, -1, -1):
+        for load in loads(chunk):
+            load.wait()
+        first = (CHUNKS - 1 - chunk) * CHUNK * GROUP
+        carry = lax.fori_loop(first, first + CHUNK * GROUP, back, carry, unroll=8)
+        out_copy(chunk).start()
+    for copy in small:
+        copy.wait()
+    for chunk in range(CHUNKS):
+        out_copy(chunk).wait()
+
+
 def per_device(nx, ny, tracers, velocity, mixing, levels, surface, transport, forcing):
     f32 = jnp.float32
     anywhere = pl.BlockSpec(memory_space=pl.ANY)
-    vmem = pl.BlockSpec(memory_space=pltpu.VMEM)
-    return pl.pallas_call(
+    held = pl.pallas_call(
         functools.partial(kernel, nx, ny),
         out_shape=(
             jax.ShapeDtypeStruct((CX, CY), f32),
             jax.ShapeDtypeStruct((2, CX, CY), f32),
             jax.ShapeDtypeStruct((2, CX, CY), f32),
             jax.ShapeDtypeStruct((2, K, CX, CY), f32),
+            jax.ShapeDtypeStruct((K, CX, CY), f32),
         ),
         in_specs=[anywhere] * 7,
-        out_specs=(vmem, vmem, vmem, anywhere),
+        out_specs=(anywhere,) * 5,
         scratch_shapes=[
             pltpu.VMEM((6, ROWS, CY), f32),
             pltpu.VMEM((2, CX, CY), f32),
@@ -406,8 +452,9 @@
             pltpu.VMEM((K, CX, CY), f32),
             pltpu.VMEM((K, CX, CY), f32),
             pltpu.VMEM((K, CX, CY), f32),
+            pltpu.VMEM((2, K, CX, CY), f32),
             pltpu.VMEM((K, CX, CY), f32),
-            pltpu.VMEM((2, K, CX, CY), f32),
+            pltpu.VMEM((2, CX, CY), f32),
             pltpu.VMEM((GROUPS, EAST_ROWS, CY), f32),
             pltpu.VMEM((GROUPS, WEST_ROWS, CY), f32),
             pltpu.VMEM((GROUPS, EAST_ROWS, CY), f32),
@@ -419,7 +466,7 @@
             pltpu.VMEM((6, 2, ROWS, CY), f32),
             pltpu.VMEM((5, 2, ROWS, CY), f32),
             pltpu.SemaphoreType.DMA((8,)),
-            pltpu.SemaphoreType.DMA((CHUNKS,)),
+            pltpu.SemaphoreType.DMA((CHUNKS + 4,)),
             pltpu.SemaphoreType.DMA((len(DIRECTIONS),)),
             pltpu.SemaphoreType.DMA((len(DIRECTIONS),)),
             pltpu.SemaphoreType.DMA((2, CHUNKS)),
@@ -428,9 +475,29 @@
             pltpu.SemaphoreType.DMA((2,)),
         ],
         compiler_params=pltpu.CompilerParams(
-            collective_id=0, has_side_effects=True, vmem_limit_bytes=40 * 1024 * 1024
+            collective_id=0, has_side_effects=True, vmem_limit_bytes=VMEM
         ),
     )(tracers, velocity, mixing, levels, surface, transport, forcing)
+    return pl.pallas_call(
+        finish,
+        out_shape=(
+            jax.ShapeDtypeStruct((CX, CY), f32),
+            jax.ShapeDtypeStruct((2, CX, CY), f32),
+            jax.ShapeDtypeStruct((2, CX, CY), f32),
+            jax.ShapeDtypeStruct((2, K, CX, CY), f32),
+        ),
+        in_specs=[anywhere] * 5,
+        out_specs=(anywhere,) * 4,
+        scratch_shapes=[
+            pltpu.VMEM((2, K, CX, CY), f32),
+            pltpu.VMEM((K, CX, CY), f32),
+            pltpu.VMEM((2, K, CX, CY), f32),
+            pltpu.SemaphoreType.DMA((3,)),
+            pltpu.SemaphoreType.DMA((2, CHUNKS)),
+            pltpu.SemaphoreType.DMA((CHUNKS,)),
+        ],
+        compiler_params=pltpu.CompilerParams(vmem_limit_bytes=VMEM),
+    )(*held)
 
 
 def solution(mesh):

time: 39.5 us -> 32.1 us (0.81)
  local copies, waits for them, and re-layouts: 9.4 us -> 0 us
  Pallas kernels: 29 us -> 31.3 us
    unnamed x18 -> x0, local copies, waits for them, and re-layouts: 9.4 us -> none
    pallas_call x0 -> x1, Pallas kernels: none -> 2.53 us  [per_device(): pl.pallas_call(finish, out_shape=(jax.ShapeDtypeStruct((CX, CY), f32), ja...]
where the time goes in v2:
time: 32.1 us; the launch traced here: 31.9 us
  Pallas kernels  31.3 us (98%)
  between operations  0.64 us (2%)
    pallas_call x1, Pallas kernels, per_device(): pl.pallas_call(functools.partial(kernel, nx, ny), out_shape=(jax.ShapeDty...  28.8 us
    pallas_call x1, Pallas kernels, per_device(): pl.pallas_call(finish, out_shape=(jax.ShapeDtypeStruct((CX, CY), f32), ja...  2.53 us

profile of v2, /device:TPU:9, one launch (start us, length us, event | category | flops | bytes accessed | tf_op | source)
XLA Modules:
  0.0 31.9 jit_solution(6367212540421757614)
XLA Ops:
  0.6 28.8 %shard_map.102 = (f32[16,128]{1,0:T(8,128)}, f32[2,16,128]{2,1,0:T(8,128)}, f32[2,16,128]{2,1,0:T(8,128)}, f32[2,80,16,128]{3,2,1,0:T(8,128)}, f32[80,16,128]{2,1,0:T(8,128)}) custom-call(f32[2,80,16,128]{3,2,1,0:T(8,128)} %tracers.1, f32[2,80,16,128]{3,2,1,0:T(8,128)} %velocity.1, f32[79,16,128]{2,1,0:T(8,128)} %mixing.1, s32[16,128]{1,0:T(8,128)} %levels.1, ...), custom_call_target="tpu_custom_call" | custom-call | tf_op jit(solution)/shard_map/pallas_call | solution.py:431
  29.4 2.5 %shard_map.103 = (f32[16,128]{1,0:T(8,128)}, f32[2,16,128]{2,1,0:T(8,128)}, f32[2,16,128]{2,1,0:T(8,128)}, f32[2,80,16,128]{3,2,1,0:T(8,128)}) custom-call(f32[16,128]{1,0:T(8,128)} %get-tuple-element.9.surface, f32[2,16,128]{2,1,0:T(8,128)} %get-tuple-element.10.transport, f32[2,16,128]{2,1,0:T(8,128)} %get-tuple-element.11.mean, ...), custom_call_target="tpu_custom_call" | custom-call | tf_op jit(solution)/shard_map/pallas_call | solution.py:481

commit v3 on v2

--- a/solution.py
+++ b/solution.py
@@ -206,7 +206,6 @@
         return upper, g
 
     zero = jnp.zeros((CX, CY), jnp.float32)
-    lax.fori_loop(0, K, factor, (zero, zero), unroll=4)
     own_state = pl.ds(OWN, CX)
     stores = [
         pltpu.make_async_copy(gain, gain_out, out_sem.at[CHUNKS]),
@@ -214,7 +213,6 @@
         pltpu.make_async_copy(state.at[1:3, 0, own_state, :], transport_out, out_sem.at[CHUNKS + 2]),
         pltpu.make_async_copy(mean, mean_out, out_sem.at[CHUNKS + 3]),
     ]
-    stores[0].start()
 
     for index, (dx, dy) in enumerate(DIRECTIONS):
         copy = barotropic_copy(index)[0]
@@ -236,11 +234,13 @@
 
     def upper_y(pair):
         a, b = (roll(x, -1, 1) for x in pair)
-        return jnp.where(wide == CY - 1, b, a), jnp.where(wide == CY - 1, a, b)
+        last = wide[: a.shape[0]] == CY - 1
+        return jnp.where(last, b, a), jnp.where(last, a, b)
 
     def lower_y(pair):
         a, b = (roll(x, 1, 1) for x in pair)
-        return jnp.where(wide == 0, b, a), jnp.where(wide == 0, a, b)
+        first = wide[: a.shape[0]] == 0
+        return jnp.where(first, b, a), jnp.where(first, a, b)
 
     depth = (fields[5], beside(5))
     east_depth = tuple(jnp.minimum(a, b) for a, b in zip(depth, upper_x(depth)))
@@ -259,27 +259,39 @@
         state[3, tile] = jnp.zeros((ROWS, CY), jnp.float32)
         state[4, tile] = jnp.zeros((ROWS, CY), jnp.float32)
 
-    def substep(step, carry):
-        east = (state[1, 0], state[1, 1])
-        north = (state[2, 0], state[2, 1])
+    def substep(low, high, levels_each, first_step, first_level, step, carry):
+        for extra in range(levels_each):
+            carry = factor(first_level + (step - first_step) * levels_each + extra, carry)
+        rows = slice(low, high)
+        east = (state[1, 0, rows, :], state[1, 1, rows, :])
+        north = (state[2, 0, rows, :], state[2, 1, rows, :])
         east_low = lower_x(east)
         north_low = lower_y(north)
         height = tuple(
-            state[0, i] - 0.5 * ((east[i] - east_low[i]) + (north[i] - north_low[i])) for i in range(2)
+            state[0, i, rows, :] - 0.5 * ((east[i] - east_low[i]) + (north[i] - north_low[i]))
+            for i in range(2)
         )
         high_x = upper_x(height)
         high_y = upper_y(height)
         for i in range(2):
-            state[0, i] = height[i]
-            e = east[i] - coef[0, i] * (high_x[i] - height[i]) + coef[1, i]
-            n = north[i] - coef[2, i] * (high_y[i] - height[i]) + coef[3, i]
-            state[1, i] = e
-            state[2, i] = n
-            state[3, i] = state[3, i] + e
-            state[4, i] = state[4, i] + n
+            state[0, i, rows, :] = height[i]
+            e = east[i] - coef[0, i, rows, :] * (high_x[i] - height[i]) + coef[1, i, rows, :]
+            n = north[i] - coef[2, i, rows, :] * (high_y[i] - height[i]) + coef[3, i, rows, :]
+            state[1, i, rows, :] = e
+            state[2, i, rows, :] = n
+            state[3, i, rows, :] = state[3, i, rows, :] + e
+            state[4, i, rows, :] = state[4, i, rows, :] + n
         return carry
 
-    lax.fori_loop(0, STEPS, substep, 0)
+    factors = (zero, zero)
+    for low, high, levels_each, first_step, first_level in (
+        (0, 72, 4, 0, 0), (8, 64, 4, 8, 32), (16, 56, 2, 16, 64),
+    ):
+        factors = lax.fori_loop(
+            first_step, first_step + 8,
+            functools.partial(substep, low, high, levels_each, first_step, first_level), factors,
+        )
+    stores[0].start()
 
     mean[0] = state[3, 0, OWN : OWN + CX, :] * (1.0 / STEPS)
     mean[1] = state[4, 0, OWN : OWN + CX, :] * (1.0 / STEPS)

time: 32.1 us -> 31.8 us (level)
    pallas_call x1, Pallas kernels: 28.8 us -> 28.4 us  [per_device(): pl.pallas_call(functools.partial(kernel, nx, ny), out_shape=(jax.ShapeDty...]
where the time goes in v3:
time: 31.8 us; the launch traced here: 31.6 us
  Pallas kernels  31 us (97%)
  between operations  0.64 us (2%)
    pallas_call x1, Pallas kernels, per_device(): pl.pallas_call(functools.partial(kernel, nx, ny), out_shape=(jax.ShapeDty...  28.4 us
    pallas_call x1, Pallas kernels, per_device(): pl.pallas_call(finish, out_shape=(jax.ShapeDtypeStruct((CX, CY), f32), ja...  2.53 us

profile of v3, /device:TPU:9, one launch (start us, length us, event | category | flops | bytes accessed | tf_op | source)
XLA Modules:
  0.0 31.6 jit_solution(14576366371474398651)
XLA Ops:
  0.6 28.4 %shard_map.102 = (f32[16,128]{1,0:T(8,128)}, f32[2,16,128]{2,1,0:T(8,128)}, f32[2,16,128]{2,1,0:T(8,128)}, f32[2,80,16,128]{3,2,1,0:T(8,128)}, f32[80,16,128]{2,1,0:T(8,128)}) custom-call(f32[2,80,16,128]{3,2,1,0:T(8,128)} %tracers.1, f32[2,80,16,128]{3,2,1,0:T(8,128)} %velocity.1, f32[79,16,128]{2,1,0:T(8,128)} %mixing.1, s32[16,128]{1,0:T(8,128)} %levels.1, ...), custom_call_target="tpu_custom_call" | custom-call | tf_op jit(solution)/shard_map/pallas_call | solution.py:443
  29.1 2.5 %shard_map.103 = (f32[16,128]{1,0:T(8,128)}, f32[2,16,128]{2,1,0:T(8,128)}, f32[2,16,128]{2,1,0:T(8,128)}, f32[2,80,16,128]{3,2,1,0:T(8,128)}) custom-call(f32[16,128]{1,0:T(8,128)} %get-tuple-element.9.surface, f32[2,16,128]{2,1,0:T(8,128)} %get-tuple-element.10.transport, f32[2,16,128]{2,1,0:T(8,128)} %get-tuple-element.11.mean, ...), custom_call_target="tpu_custom_call" | custom-call | tf_op jit(solution)/shard_map/pallas_call | solution.py:493
